TPU v7x, 256 devices: a whole 4x4x8 slice. The times are simulated.
256 devices in a mesh: ctx: 32 (over z, x_hi, core), head: 8 (over y, x_lo).
Axes of the slice: x: 4 (x_hi: 2, x_lo: 2; x = x_hi * 2 + x_lo), y: 4, z: 8, core: 2. Of those that a mesh axis runs over, the one named last changes fastest.
Arguments:
- queries: bfloat16 [4096, 64, 192], P('ctx', 'head'), may hold values from -8 to 8
- latent: bfloat16 [4096, 512], P('ctx'), may hold values from -6 to 6
- key_rope: bfloat16 [4096, 64], P('ctx'), may hold values from -8 to 8
- up_keys: bfloat16 [512, 64, 128], P(None, 'head'), may hold values from -0.25 to 0.25
- up_values: bfloat16 [512, 64, 128], P(None, 'head'), may hold values from -0.25 to 0.25
- out_weight: bfloat16 [8192, 7168], P('head', 'ctx'), may hold values from -1 to 1
- block_order: int32 [64], replicated, may hold values from 0 to 63, each once
Outputs:
- mixed: bfloat16 [4096, 7168], P('ctx', 'head')
Inputs may be any that keep to these rules, and one draw needn't show every extreme that they name: A permutation; row r of the prompt lies in position block block_order[r // 64].
All inputs are finite; a program needn't handle non-finite values.
Results may differ from a plain program's by a relative error of at most 0.019.
Values may be sent and summed in bfloat16 or wider, within the bound.
A program may use at most 128 MiB of HBM per device.

v0:
```python
import jax
import jax.numpy as jnp
from jax import lax
from jax.sharding import PartitionSpec as P


def token_positions(indices, block_order, half_rows):
    block_ids = indices // half_rows
    table = (
        block_ids[:, None] == jnp.arange(block_order.shape[0], dtype=jnp.int32)[None, :]
    ).astype(jnp.int32)
    starts = jnp.sum(table * block_order[None, :], axis=1)
    return starts * half_rows + indices % half_rows


def shards(queries, latent, key_rope, up_keys, up_values, out_weight, block_order):
    row_count = queries.shape[0]
    head_count = queries.shape[1]
    latent_width = up_keys.shape[0]
    nope_dims = up_keys.shape[2]
    value_dims = up_values.shape[2]
    half_rows = row_count // 2
    scale = queries.shape[2] ** (-0.5)
    my_index = lax.axis_index("ctx")
    query_pos = token_positions(
        my_index * row_count + jnp.arange(row_count, dtype=jnp.int32), block_order, half_rows
    )
    keys_flat = up_keys.reshape(latent_width, head_count * nope_dims)
    values_flat = up_values.reshape(latent_width, head_count * value_dims)
    query_nope = queries[:, :, :nope_dims]
    query_rope = queries[:, :, nope_dims:]
    lat_piece = lax.all_gather(latent, "ctx", axis=0, tiled=True)
    rope_piece = lax.all_gather(key_rope, "ctx", axis=0, tiled=True)
    piece_rows = lat_piece.shape[0]
    key_pos = token_positions(jnp.arange(piece_rows, dtype=jnp.int32), block_order, half_rows)
    visible = key_pos[None, :] <= query_pos[:, None]
    run_max = jnp.full((head_count, row_count), -1e30, jnp.float32)
    keys_nope = jnp.dot(lat_piece, keys_flat, preferred_element_type=jnp.float32).astype(
        jnp.bfloat16
    )
    keys_nope = keys_nope.reshape(piece_rows, head_count, nope_dims)
    values = jnp.dot(lat_piece, values_flat, preferred_element_type=jnp.float32).astype(
        jnp.bfloat16
    )
    values = values.reshape(piece_rows, head_count, value_dims)
    scores = jnp.einsum("qhd,khd->hqk", query_nope, keys_nope, preferred_element_type=jnp.float32)
    scores = scores + jnp.einsum(
        "qhd,kd->hqk", query_rope, rope_piece, preferred_element_type=jnp.float32
    )
    scores = jnp.where(visible[None, :, :], scores * scale, -1e30)
    new_max = jnp.maximum(run_max, jnp.max(scores, axis=2))
    powers = jnp.exp(scores - new_max[:, :, None])
    new_sum = jnp.sum(powers, axis=2)
    added = jnp.einsum(
        "hqk,khe->qhe", powers.astype(jnp.bfloat16), values, preferred_element_type=jnp.float32
    )
    attended = (
        (added / jnp.transpose(new_sum)[:, :, None])
        .astype(jnp.bfloat16)
        .reshape(row_count, head_count * value_dims)
    )
    partial_out = jnp.dot(
        attended,
        lax.all_gather(out_weight, "ctx", axis=1, tiled=True),
        preferred_element_type=jnp.float32,
    )
    return lax.psum_scatter(
        partial_out.astype(jnp.bfloat16), "head", scatter_dimension=1, tiled=True
    )


def solution(mesh):
    placed = (
        P("ctx", "head", None),
        P("ctx", None),
        P("ctx", None),
        P(None, "head", None),
        P(None, "head", None),
        P("head", "ctx"),
        P(),
    )
    return jax.shard_map(
        shards, mesh=mesh, in_specs=placed, out_specs=P("ctx", "head"), check_vma=False
    )
```

profile of v0, /device:TPU:17, one launch (start us, length us, event | category | flops | bytes accessed | tf_op | source)
XLA Modules:
  0.0 292.7 jit_solution(7846370537295553673)
XLA Ops:
  6.5 0.0 all-gather.3.cloned.1.call-start
  6.5 0.7 all-gather.3.cloned.1.call-update
  7.3 0.0 all-gather.5.cloned.1.call-start
  7.3 0.7 all-gather.5.cloned.1.call-update
  8.0 0.0 reduce-scatter.4.cloned.1.call-start
  8.1 0.7 select_reduce_fusion.1
  8.8 0.9 select_reduce_fusion
  9.8 47.0 %all_gather.10 = bf16[4096,64]{0,1:T(8,128)(2,1)S(1)} all-gather(bf16[128,64]{0,1:T(8,128)(2,1)} %param.9), channel_id=1, replica_groups=mesh['ctx'=32,'head'=8] {'ctx'}, dimensions={0}, use_global_device_ids=true | all-gather | bytes 540672 | tf_op jit(solution)/shard_map/all_gather | solution.py:33
  56.7 1.8 broadcast_compare_fusion
  58.6 41.6 %all-gather.3.cloned.1.call-done = bf16[4096,512]{1,0:T(8,128)(2,1)} async-done(((bf16[128,512]{1,0:T(8,128)(2,1)}), bf16[4096,512]{1,0:T(8,128)(2,1)}) %all-gather.3.cloned.1.call-update) | async-done | bytes 4194320 | tf_op jit(solution)/shard_map/all_gather | solution.py:32
  100.2 0.0 copy-start
  100.2 10.3 %convolution_convert_fusion.1 = bf16[4096,1024]{0,1:T(8,128)(2,1)} fusion(bf16[4096,512]{1,0:T(8,128)(2,1)} %all-gather.3.cloned.1.call-done, bf16[64,8,8,128]{3,2,1,0:T(8,128)(2,1)} %bitcast.45), kind=kOutput, calls=%fused_computation.9 | convolution fusion | flops 4299161600 | bytes 13631488 | tf_op jit(solution)/shard_map/dot_general | solution.py:38
  110.5 0.0 copy-done
  110.5 12.2 %fusion.21 = f32[8,4096,128]{2,1,0:T(8,128)} fusion(bf16[4096,8,128]{0,2,1:T(8,128)(2,1)} %bitcast.39, bf16[128,8,192]{0,2,1:T(8,128)(2,1)S(1)} %copy-done), kind=kOutput, calls=%fused_computation.22 | convolution fusion | flops 1073741824 | bytes 25427968 | tf_op jit(solution)/shard_map/qhd,khd->hqk/dot_general | solution.py:46
  122.7 10.9 %fusion.33 = (f32[8,128]{1,0:T(8,128)S(1)}, f32[8,128,4096]{1,2,0:T(8,128)}) fusion(bf16[128,8,192]{0,2,1:T(8,128)(2,1)S(1)} %copy-done, bf16[4096,64]{0,1:T(8,128)(2,1)S(1)} %all_gather.10, f32[8,4096,128]{2,1,0:T(8,128)} %fusion.21, pred[128,4096]{0,1:T(8,128)(4,1)S(1)} %broadcast_compare_fusion), kind=kOutput, calls=%fused_computation.47 | convolution fusion | flops 553647104 | bytes 34738176 | tf_op jit(solution)/shard_map/qhd,kd->hqk/dot_general | solution.py:47
  133.6 0.0 copy-start.1
  133.6 8.2 %fusion.2 = f32[8,128]{1,0:T(8,128)S(1)} fusion(f32[8,128,4096]{1,2,0:T(8,128)} %get-tuple-element.6, f32[8,128]{1,0:T(8,128)S(1)} %broadcast_maximum_fusion), kind=kLoop, calls=%fused_computation.4 | loop fusion | flops 8387584 | bytes 16785408 | tf_op jit(solution)/shard_map/reduce_sum | solution.py:53
  141.8 0.0 copy-done.1
  141.8 7.2 %convolution_convert_fusion.2 = bf16[4096,1024]{0,1:T(8,128)(2,1)S(1)} fusion(bf16[4096,512]{1,0:T(8,128)(2,1)} %all-gather.3.cloned.1.call-done, bf16[64,8,8,128]{3,2,1,0:T(8,128)(2,1)S(1)} %bitcast.46), kind=kOutput, calls=%fused_computation.10 | convolution fusion | flops 4299161600 | bytes 13631488 | tf_op jit(solution)/shard_map/dot_general | solution.py:42
  149.0 11.0 %fusion.13 = bf16[128,8,128]{0,2,1:T(8,128)(2,1)S(1)} fusion(bf16[4096,8,128]{0,2,1:T(8,128)(2,1)S(1)} %bitcast.40, f32[8,128,4096]{1,2,0:T(8,128)} %get-tuple-element.6, f32[8,128]{1,0:T(8,128)S(1)} %broadcast_maximum_fusion, f32[128,8]{0,1:T(8,128)S(1)} %bitcast.44), kind=kOutput, calls=%fused_computation.13 | convolution fusion | flops 1082392576 | bytes 25436160 | tf_op jit(solution)/shard_map/hqk,khe->qhe/dot_general | solution.py:54
  160.0 67.0 %all-gather.5.cloned.1.call-done = bf16[1024,7168]{0,1:T(8,128)(2,1)} async-done(((bf16[1024,224]{0,1:T(8,128)(2,1)}), bf16[1024,7168]{0,1:T(8,128)(2,1)}) %all-gather.5.cloned.1.call-update) | async-done | bytes 14680080 | tf_op jit(solution)/shard_map/all_gather | solution.py:64
  227.0 10.1 %convolution_convert_fusion = bf16[128,7168]{1,0:T(8,128)(2,1)S(1)} fusion(bf16[128,1024]{0,1:T(8,128)(2,1)S(1)} %bitcast.42, bf16[1024,7168]{0,1:T(8,128)(2,1)} %all-gather.5.cloned.1.call-done), kind=kOutput, calls=%fused_computation.6 | convolution fusion | flops 1879965696 | bytes 16777216 | tf_op jit(solution)/shard_map/dot_general | solution.py:62
  237.1 2.3 copy.19
  239.5 0.0 reduce-scatter.4.cloned.1.call-update
  239.5 44.9 %reduce-scatter.4.cloned.1.call-done = bf16[896,128]{1,0:T(8,128)(2,1)} async-done(((bf16[7168,128]{1,0:T(8,128)(2,1)}), bf16[896,128]{1,0:T(8,128)(2,1)}) %reduce-scatter.4.cloned.1.call-update) | async-done | bytes 229392
  284.4 1.8 copy.20
  (5 shorter events, 0.0 us)
Async XLA Ops:
  6.5 93.6 %all-gather.3.cloned.1.call-start = ((), (), s32[]{:S(2)}) async-start(), calls=%async_computation.1 | async-start | bytes 4325376 | tf_op jit(solution)/shard_map/all_gather | solution.py:32
  7.3 219.7 %all-gather.5.cloned.1.call-start = ((), (), s32[]{:S(2)}) async-start(), calls=%async_computation.2 | async-start | bytes 15138816 | tf_op jit(solution)/shard_map/all_gather | solution.py:64
  8.0 276.4 %reduce-scatter.4.cloned.1.call-start = ((), (), s32[]{:S(2)}) async-start(), calls=%async_computation.3 | async-start | bytes 2064384
  100.2 10.3 %copy-start = (bf16[128,8,192]{0,2,1:T(8,128)(2,1)S(1)}, bf16[128,8,192]{0,2,1:T(8,128)(2,1)}, u32[]{:S(2)}) copy-start(bf16[128,8,192]{0,2,1:T(8,128)(2,1)} %param.7) | copy-start | bytes 1179652
  133.6 8.2 %copy-start.1 = (bf16[512,8,128]{2,1,0:T(8,128)(2,1)S(1)}, bf16[512,8,128]{2,1,0:T(8,128)(2,1)}, u32[]{:S(2)}) copy-start(bf16[512,8,128]{2,1,0:T(8,128)(2,1)} %param.11) | copy-start | bytes 3145732
Sparse Core Ops, SparseCore 0:
  10.1 89.9 all-gather.2
  102.9 124.0 all-gather.4
  239.6 44.7 reduce-scatter.3
where the time goes:
time: 296 us; the launch traced here: 293 us
  waiting for transfers between devices  155 us (52%)
  matrix products  61.8 us (21%)
  blocking collectives  47 us (16%)
  between operations  13.2 us (4%)
  other arithmetic  11.7 us (4%)
  local copies, waits for them, and re-layouts  4.1 us (1%)
    all_gather x1, waiting for transfers between devices, shards(): lax.all_gather(out_weight, 'ctx', axis=1, tiled=True)  67 us
    all_gather x1, blocking collectives, shards(): rope_piece = lax.all_gather(key_rope, 'ctx', axis=0, tiled=True)  47 us
    unnamed x4, waiting for transfers between devices  46.3 us
    all_gather x1, waiting for transfers between devices, shards(): lat_piece = lax.all_gather(latent, 'ctx', axis=0, tiled=True)  41.6 us
    dot_general x1, matrix products, shards(): jnp.einsum('qhd,khd->hqk', query_nope, keys_nope, preferred_element_type=...  12.2 us
    dot_general x1, matrix products, shards(): jnp.einsum('hqk,khe->qhe', powers.astype(jnp.bfloat16), values, preferred...  11 us
    dot_general x1, matrix products, shards(): jnp.einsum('qhd,kd->hqk', query_rope, rope_piece, preferred_element_type=...  10.9 us
    dot_general x1, matrix products, shards(): jnp.dot(lat_piece, keys_flat, preferred_element_type=jnp.float32)  10.3 us
  transfers between devices with their start and end apart: 3, of which 3 were waited for; matrix products, arithmetic and copies ran while one was open for 22% of the time, Pallas kernels for 0%

commit v1 on v0

v1 whole, which is shorter than its diff:
```python
import functools

import jax
import jax.numpy as jnp
from jax import lax
from jax.experimental import pallas as pl
from jax.experimental.pallas import tpu as pltpu
from jax.sharding import PartitionSpec as P

MESH = pl.DeviceIdType.MESH
F32 = jnp.float32
BF16 = jnp.bfloat16
NT = (((1,), (1,)), ((), ()))
LOW = -1e30


def wait(ref, sem):
    pltpu.make_async_copy(ref, ref, sem).wait()


def kernel(
    q_ref, lat_ref, rope_ref, uk_ref, uv_ref, w_ref, order_ref, out_ref,
    lat, keys, qp, bias, acc, top, total, w_in, w1, w2, att, part, got, summed, turned, final,
    x_sem, w_sem, lz_send, lz_recv, ls_send, ls_recv, az_send, az_recv, as_send, as_recv,
    c_send, c_recv, t_send, t_recv, f_send, f_recv,
):
    ctx, head = lax.axis_index("ctx"), lax.axis_index("head")
    z, xh, core = ctx // 4, (ctx // 2) % 2, ctx % 2
    y, xl = head // 2, head % 2
    factor = (192.0 ** -0.5) * 1.4426950408889634

    def at(z_, xh_, core_, y_, xl_):
        return (z_ * 4 + xh_ * 2 + core_, y_ * 2 + xl_)

    sibling = at(z, xh, 1 - core, y, xl)
    x_next = at(z, 1 - xh, core, y, 1 - xl)
    x_far = at(z, 1 - xh, core, y, xl)

    def send(src, dst, send_sem, recv_sem, device):
        pltpu.make_async_remote_copy(
            src_ref=src, dst_ref=dst, send_sem=send_sem, recv_sem=recv_sem,
            device_id=device, device_id_type=MESH,
        ).start()

    def other_head(step, core_):
        return at(z, xh, core_, (y + step // 2) % 4, (xl + step) % 2)

    barrier = pltpu.get_barrier_semaphore()
    partners = [sibling, x_next, x_far]
    partners += [at((z + step) % 8, xh, core, y, xl) for step in range(1, 8)]
    partners += [other_head(step, c) for step in range(1, 8) for c in (core, 1 - core)]
    for device in partners:
        pl.semaphore_signal(barrier, inc=1, device_id=device, device_id_type=MESH)

    lat[z, core, xh, 0:128, :] = lat_ref[...]
    rope = rope_ref[...].astype(F32)
    rope = rope[0:64, :] + pltpu.roll(rope[64:128, :], 64, 1)
    for g in range(4):
        lat[z, core, xh, 128:144, g * 128 : (g + 1) * 128] = rope[g * 16 : (g + 1) * 16, :].astype(BF16)

    pl.semaphore_wait(barrier, len(partners))
    mine = lat.at[z, core, xh]
    send(mine, mine, x_sem.at[0], x_sem.at[1], x_next)

    def project(h, carry):
        rows = pl.ds(pl.multiple_of(h * 128, 128), 128)
        qp[rows, 0:512] = lax.dot_general(
            q_ref[h, :, 0:128], uk_ref[h], NT, preferred_element_type=F32
        ).astype(BF16)
        qp[rows, 512:640] = q_ref[h, :, 128:256]
        return carry

    lax.fori_loop(0, 8, project, 0)
    top[...] = jnp.full_like(top, LOW)
    total[...] = jnp.zeros_like(total)
    acc[...] = jnp.zeros_like(acc)
    wait(mine, x_sem.at[1])

    def ring(buf, s, side, z_send, z_recv, s_send, s_recv):
        zz = (z + 8 - s) % 8 if side == 0 else (z + s) % 8
        block = buf.at[zz, core]
        active = (s >= 0) if side == 0 else ((s >= 1) & (s <= 3))

        @pl.when(active & (s > 0))
        def _():
            wait(block, z_recv.at[zz])

        @pl.when((s < 3) | ((s == 3) & (core == side)))
        def _():
            to = (z + 1) % 8 if side == 0 else (z + 7) % 8
            send(block, block, z_send.at[0], z_recv.at[zz], at(to, xh, core, y, xl))

        @pl.when(active)
        def _():
            send(block, block, s_send.at[0], s_recv.at[zz], sibling)

        return zz, active

    lane = lax.broadcasted_iota(jnp.int32, (128, 512), 1)
    row = lax.broadcasted_iota(jnp.int32, (128, 512), 0)

    def attend(zz):
        wait(lat.at[zz, 1 - core], ls_recv.at[zz])
        place = jnp.zeros((128, 512), jnp.int32)
        for c in range(2):
            for x in range(2):
                n = c * 2 + x
                for half in range(2):
                    block = order_ref[zz * 8 + x * 4 + c * 2 + half] * 64
                    place = jnp.where(lane // 64 == n * 2 + half, block + lane % 64, place)
                keys[n * 128 : (n + 1) * 128, 0:512] = lat[zz, c, x, 0:128, :]
                for g in range(4):
                    pair = lat[zz, c, x, 128:144, g * 128 : (g + 1) * 128]
                    keys[n * 128 + g * 16 : n * 128 + g * 16 + 16, 512:640] = pair
                    turn = pltpu.roll(pair.astype(F32), 64, 1).astype(BF16)
                    keys[n * 128 + 64 + g * 16 : n * 128 + 64 + g * 16 + 16, 512:640] = turn
        own = jnp.where(
            row < 64, order_ref[ctx * 2] * 64 + row, order_ref[ctx * 2 + 1] * 64 + row - 64
        )
        bias[...] = jnp.where(place <= own, 0.0, LOW)
        for r in range(4):
            rows = slice(r * 256, (r + 1) * 256)
            s = lax.dot_general(qp[rows, :], keys[...], NT, preferred_element_type=F32)
            s = s + jnp.concatenate([bias[...], bias[...]], axis=0)
            old = top[rows, :]
            new = jnp.maximum(old, jnp.max(s, axis=1, keepdims=True))
            top[rows, :] = new
            p = jnp.exp2((s - new[:, 0:1]) * factor)
            fade = jnp.exp2((old - new) * factor)
            total[rows, :] = total[rows, :] * fade + (
                (p[:, 0:128] + p[:, 128:256]) + (p[:, 256:384] + p[:, 384:512])
            )
            added = jnp.dot(p.astype(BF16), keys[:, 0:512], preferred_element_type=F32)
            acc[rows, :] = acc[rows, :] * fade[:, 0:1] + added

    def gather_step(s, carry):
        z0, on0 = ring(lat, s, 0, lz_send, lz_recv, ls_send, ls_recv)
        z1, on1 = ring(lat, s, 1, lz_send, lz_recv, ls_send, ls_recv)

        @pl.when(s == 1)
        def _():
            send(w_ref, w_in, w_sem.at[0], w_sem.at[1], x_far)

        def one(i, c):
            attend(jnp.where(i == 0, z0, z1))
            return c

        lax.fori_loop(0, jnp.where((s >= 1) & (s <= 3), 2, 1), one, 0)
        return carry

    lax.fori_loop(0, 5, gather_step, 0)

    wait(w_in, w_sem.at[1])

    def widen(i, carry):
        rows = pl.ds(pl.multiple_of(i * 128, 128), 128)
        held, came = w_ref[rows, :].astype(F32), w_in[rows, :].astype(F32)
        first = jnp.where(xh == 0, held, came)
        second = jnp.where(xh == 0, came, held)
        empty = jnp.zeros((128, 256), F32)
        wide = jnp.concatenate([first, empty], axis=1) + pltpu.roll(
            jnp.concatenate([second, empty], axis=1), 224, 1
        )
        w1[rows, :] = wide.astype(BF16)
        w2[rows, :] = pltpu.roll(wide, 64, 1).astype(BF16)
        return carry

    lax.fori_loop(0, 8, widen, 0)

    def finish(h, carry):
        rows = pl.ds(pl.multiple_of(h * 128, 128), 128)
        mean = acc[rows, :] / jnp.sum(total[rows, :], axis=1, keepdims=True)
        att[z, core, :, rows] = jnp.dot(
            mean.astype(BF16), uv_ref[h], preferred_element_type=F32
        ).astype(BF16)
        return carry

    lax.fori_loop(0, 8, finish, 0)

    def multiply(zz):
        wait(att.at[zz, 1 - core], as_recv.at[zz])
        a = jnp.dot(att[zz, 0], w1[...], preferred_element_type=F32)
        b = jnp.dot(att[zz, 1], w2[...], preferred_element_type=F32)
        part[zz, :, 0:384] = a[:, 0:384].astype(BF16)
        part[zz, :, 384:512] = (a[:, 384:512] + b[:, 0:128]).astype(BF16)
        part[zz, :, 512:896] = b[:, 128:512].astype(BF16)
        for step in range(1, 8):
            y_, xl_ = (y + step // 2) % 4, (xl + step) % 2
            rows = pl.ds(pl.multiple_of((y_ * 2 + xl_) * 16, 16), 16)
            send(
                part.at[zz, rows], got.at[zz, head], c_send.at[0], c_recv.at[zz],
                at(z, xh, core, y_, xl_),
            )
        rows = pl.ds(pl.multiple_of(head * 16, 16), 16)
        got[zz, head] = part[zz, rows, :]

    def reduce(zz):
        wait(got.at[zz, 0:7], c_recv.at[zz])
        whole = got[zz, 0].astype(F32)
        for h in range(1, 8):
            whole = whole + got[zz, h].astype(F32)

        @pl.when(zz == z)
        def _():
            turned[z] = whole.astype(BF16)

        @pl.when(zz != z)
        def _():
            summed[zz] = whole.astype(BF16)
            send(
                summed.at[zz], turned.at[z], t_send.at[0], t_recv.at[z],
                at(zz, xh, core, y, xl),
            )

    def deliver(zz):
        @pl.when(zz != z)
        def _():
            wait(turned.at[zz], t_recv.at[zz])

        for c in range(2):
            window = slice(384 * c, 384 * c + 512)
            own = (zz == head) & (core == c)

            @pl.when(own)
            def _():
                final[head * 2 + core] = turned[zz, :, window]

            @pl.when(jnp.logical_not(own))
            def _():
                send(
                    turned.at[zz, :, window], final.at[head * 2 + core],
                    f_send.at[0], f_recv.at[0], at(z, xh, c, zz // 2, zz % 2),
                )

    def pair(s, work):
        def one(i, c):
            work(jnp.where(i == 0, (z + 8 - s) % 8, (z + s) % 8))
            return c

        lax.fori_loop(0, jnp.where((s >= 1) & (s <= 3), 2, 1), one, 0)

    def output_step(s, carry):
        @pl.when(s <= 4)
        def _():
            ring(att, s, 0, az_send, az_recv, as_send, as_recv)
            ring(att, s, 1, az_send, az_recv, as_send, as_recv)
            pair(s, multiply)

        @pl.when((s >= 1) & (s <= 5))
        def _():
            pair(s - 1, reduce)

        @pl.when(s >= 2)
        def _():
            pair(s - 2, deliver)

        return carry

    lax.fori_loop(0, 7, output_step, 0)

    wait(final.at[0:15], f_recv.at[0])
    for c in range(2):

        @pl.when(core == c)
        def _():
            def place(h, carry):
                rows = pl.ds(pl.multiple_of(h * 16, 16), 16)
                v0, v1 = final[h * 2].astype(F32), final[h * 2 + 1].astype(F32)
                empty = jnp.zeros((16, 512), F32)
                v0 = jnp.concatenate([v0, empty], axis=1)
                v1 = jnp.concatenate([v1, empty], axis=1)
                back = 64 * c
                column = lax.broadcasted_iota(jnp.int32, (16, 1024), 1)

                def turn(v, by):
                    return v if by % 1024 == 0 else pltpu.roll(v, by % 1024, 1)

                full = jnp.where(
                    column < 448,
                    jnp.where(column < 224, turn(v0, -back), turn(v1, 224 - back)),
                    jnp.where(column < 672, turn(v0, 224 - back), turn(v1, 448 - back)),
                )
                out_ref[rows, :] = full[:, 0:896].astype(BF16)
                return carry

            lax.fori_loop(0, 8, place, 0)

    wait(mine, x_sem.at[0])
    wait(w_in, w_sem.at[0])
    wait(lat.at[0:7, 0], lz_send.at[0])
    wait(lat.at[0:8, 0], ls_send.at[0])
    wait(att.at[0:7, 0], az_send.at[0])
    wait(att.at[0:8, 0], as_send.at[0])
    wait(part.at[0:7], c_send.at[0])
    wait(summed.at[0:7], t_send.at[0])
    wait(final.at[0:15], f_send.at[0])


def shards(queries, latent, key_rope, up_keys, up_values, out_weight, block_order):
    q = jnp.pad(jnp.transpose(queries, (1, 0, 2)), ((0, 0), (0, 0), (0, 64)))
    uk = jnp.transpose(up_keys, (1, 0, 2))
    uv = jnp.transpose(up_values, (1, 0, 2))
    w = jnp.pad(out_weight, ((0, 0), (0, 32)))
    rope = jnp.pad(key_rope, ((0, 0), (0, 64)))
    vmem = pl.BlockSpec(memory_space=pltpu.VMEM)
    smem = pl.BlockSpec(memory_space=pltpu.SMEM)
    dma = pltpu.SemaphoreType.DMA
    return pl.pallas_call(
        kernel,
        out_shape=jax.ShapeDtypeStruct((128, 896), BF16),
        in_specs=[vmem] * 6 + [smem],
        out_specs=vmem,
        scratch_shapes=[
            pltpu.VMEM((8, 2, 2, 144, 512), BF16),
            pltpu.VMEM((512, 640), BF16),
            pltpu.VMEM((1024, 640), BF16),
            pltpu.VMEM((128, 512), F32),
            pltpu.VMEM((1024, 512), F32),
            pltpu.VMEM((1024, 128), F32),
            pltpu.VMEM((1024, 128), F32),
            pltpu.VMEM((1024, 256), BF16),
            pltpu.VMEM((1024, 512), BF16),
            pltpu.VMEM((1024, 512), BF16),
            pltpu.VMEM((8, 2, 128, 1024), BF16),
            pltpu.VMEM((8, 128, 896), BF16),
            pltpu.VMEM((8, 8, 16, 896), BF16),
            pltpu.VMEM((8, 16, 896), BF16),
            pltpu.VMEM((8, 16, 896), BF16),
            pltpu.VMEM((16, 16, 512), BF16),
            dma((2,)), dma((2,)),
            dma((1,)), dma((8,)), dma((1,)), dma((8,)),
            dma((1,)), dma((8,)), dma((1,)), dma((8,)),
            dma((1,)), dma((8,)),
            dma((1,)), dma((8,)),
            dma((1,)), dma((1,)),
        ],
        compiler_params=pltpu.CompilerParams(
            collective_id=0, has_side_effects=True, vmem_limit_bytes=56 * 2**20
        ),
        cost_estimate=pl.CostEstimate(
            flops=25 * 10**9, bytes_accessed=4 * 2**20, transcendentals=4 * 2**20
        ),
        name="latent_attention",
    )(q, latent, rope, uk, uv, w, block_order)


def solution(mesh):
    placed = (
        P("ctx", "head", None),
        P("ctx", None),
        P("ctx", None),
        P(None, "head", None),
        P(None, "head", None),
        P("head", "ctx"),
        P(),
    )
    return jax.shard_map(
        shards, mesh=mesh, in_specs=placed, out_specs=P("ctx", "head"), check_vma=False
    )
```

time: 296 us -> 107 us (0.36)
  waiting for transfers between devices: 155 us -> 0 us
  Pallas kernels: 0 us -> 98.1 us
  matrix products: 61.8 us -> 0 us
  blocking collectives: 47 us -> 0 us
  between operations: 13.2 us -> 0.03 us
  other arithmetic: 11.7 us -> 0 us
  local copies, waits for them, and re-layouts: 4.1 us -> 8.26 us
    all_gather x2 -> x0, waiting for transfers between devices: 109 us -> none  [the longest x1 67 us: shards(): lax.all_gather(out_weight, 'ctx', axis=1, tiled=True)]
    pallas_call x0 -> x1, Pallas kernels: none -> 98.1 us  [shards(): pl.pallas_call(kernel, out_shape=jax.ShapeDtypeStruct((128, 896), BF16),...]
    dot_general x6 -> x0, matrix products: 61.8 us -> none  [the longest x1 12.2 us: shards(): jnp.einsum('qhd,khd->hqk', query_nope, keys_nope, preferred_element_type=...]
    all_gather x1 -> x0, blocking collectives: 47 us -> none  [shards(): rope_piece = lax.all_gather(key_rope, 'ctx', axis=0, tiled=True)]
    unnamed x4 -> x0, waiting for transfers between devices: 46.3 us -> none
    reduce_sum x3 -> x0, other arithmetic: 9.85 us -> none  [the longest x1 8.2 us: shards(): new_sum = jnp.sum(powers, axis=2)]
  transfers between devices with their start and end apart: 3 -> 0, of which waited for: 3 -> 0; matrix products, arithmetic and copies ran while one was open for 22% -> 0% of each run, Pallas kernels for 0% -> 0%
where the time goes in v1:
time: 107 us; the launch traced here: 106 us
  Pallas kernels  98.1 us (92%)
  local copies, waits for them, and re-layouts  8.26 us (8%)
    pallas_call x1, Pallas kernels, shards(): pl.pallas_call(kernel, out_shape=jax.ShapeDtypeStruct((128, 896), BF16),...  98.1 us
    unnamed x10, local copies, waits for them, and re-layouts  4.12 us

profile of v1, /device:TPU:17, one launch (start us, length us, event | category | flops | bytes accessed | tf_op | source)
XLA Modules:
  0.0 106.4 jit_solution(13882378330047352735)
XLA Ops:
  0.0 0.8 copy.9
  0.8 0.6 pad.13.rope_ref
  1.5 0.0 copy-start.2
  1.5 1.3 %copy.8 = bf16[128,8,192]{2,0,1:T(8,128)(2,1)S(1)} copy(bf16[128,8,192]{0,2,1:T(8,128)(2,1)} %param.7) | data formatting | bytes 786432 | tf_op args[0]
  2.7 0.0 copy-start.1
  2.7 0.9 pad.12.q_ref
  3.6 0.0 copy-done.2
  3.6 0.0 copy-start
  3.6 0.2 copy.12
  3.8 0.9 pad.14.w_ref
  4.7 0.0 copy-done.1
  4.7 0.2 copy-done
  4.9 1.7 %copy_bitcast_fusion = (bf16[8,512,128]{2,1,0:T(8,128)(2,1)}, bf16[8,512,128]{2,1,0:T(8,128)(2,1)}) fusion(bf16[512,8,128]{2,1,0:T(8,128)(2,1)S(1)} %copy-done, bf16[512,8,128]{2,1,0:T(8,128)(2,1)S(1)} %copy-done.1), kind=kLoop, calls=%fused_computation | loop fusion | bytes 4194304 | tf_op jit(solution)/shard_map/transpose | solution.py:302
  6.6 98.1 %latent_attention.1 = bf16[128,896]{1,0:T(8,128)(2,1)} custom-call(bf16[8,128,256]{2,1,0:T(8,128)(2,1)} %pad.12.q_ref, bf16[128,512]{1,0:T(8,128)(2,1)} %lat_ref.1, bf16[128,128]{1,0:T(8,128)(2,1)} %pad.13.rope_ref, bf16[8,512,128]{2,1,0:T(8,128)(2,1)} %get-tuple-element.6.uk_ref, bf16[8,512,128]{2,1,0:T(8,128)(2,1)} %get-tuple-element.5.uv_ref, ...), custom_call_target="tpu_custom_call" | custom-call | flops 24999999488 | bytes 4194304 | tf_op jit(solution)/shard_map/latent_attention/pallas_call | solution.py:308
  104.8 1.6 %copy.16 = bf16[128,896]{1,0:T(8,128)(2,1)} copy(bf16[128,896]{1,0:T(8,128)(2,1)} %latent_attention.1) | data formatting | bytes 458752
Async XLA Ops:
  1.5 2.2 %copy-start.2 = (bf16[1024,224]{0,1:T(8,128)(2,1)S(1)}, bf16[1024,224]{0,1:T(8,128)(2,1)}, u32[]{:S(2)}) copy-start(bf16[1024,224]{0,1:T(8,128)(2,1)} %param.12) | copy-start | bytes 1376260
  2.7 2.0 %copy-start.1 = (bf16[512,8,128]{2,1,0:T(8,128)(2,1)S(1)}, bf16[512,8,128]{2,1,0:T(8,128)(2,1)}, u32[]{:S(2)}) copy-start(bf16[512,8,128]{2,1,0:T(8,128)(2,1)} %param.10) | copy-start | bytes 3145732
  3.6 1.3 %copy-start = (bf16[512,8,128]{2,1,0:T(8,128)(2,1)S(1)}, bf16[512,8,128]{2,1,0:T(8,128)(2,1)}, u32[]{:S(2)}) copy-start(bf16[512,8,128]{2,1,0:T(8,128)(2,1)} %param.11) | copy-start | bytes 3145732
